TPU v7x, 256 devices: a whole 4x4x8 slice. The times are simulated.
256 devices in a mesh: list: 32 (over z_lo, y, core), tensor: 8 (over x, z_hi).
Axes of the slice: x: 4, y: 4, z: 8 (z_hi: 2, z_lo: 4; z = z_hi * 4 + z_lo), core: 2. Of those that a mesh axis runs over, the one named last changes fastest.
Arguments:
- states: bfloat16 [768, 16, 4096], P('list', None, 'tensor')
- lengths: int32 [768], P('list'), may hold values from 2 to 16, as said below
- assign: int32 [768], P('list'), may hold values from 0 to 131071, as said below
- norm_gain: float32 [4096], replicated, may hold values from 0.1 to 1.9
- gate_weight: bfloat16 [4096, 7168], P('list', 'tensor'), may hold values from -0.09375 to 0.09375
- up_weight: bfloat16 [4096, 7168], P('list', 'tensor'), may hold values from -0.09375 to 0.09375
- down_weight: bfloat16 [7168, 4096], P('tensor', 'list'), may hold values from -0.0625 to 0.0625
- out_gain: float32 [4096], P('tensor'), may hold values from 0.25 to 1.75
- centroids: bfloat16 [131072, 4096], P('list', 'tensor'), may hold values from -6 to 6
Outputs:
- embedding: float32 [768, 4096], P('list', 'tensor')
- residual: float32 [768, 4096], P('list', 'tensor')
Inputs may be any that keep to these rules, and one draw needn't show every extreme that they name: `lengths`: some passage has all 16 slots filled in every draw. `assign`: centroids of index o of list are rows o * 4096 to (o + 1) * 4096 - 1. Of the 24 passages of one index of list at most 2 are assigned to centroids of any one index of list, and in every draw some index of list is assigned exactly 2 passages by every index of list.
All inputs are finite; a program needn't handle non-finite values.
Results may differ from a plain program's by a relative error of at most 0.0065.
Values may be sent and summed in bfloat16 or wider, within the bound.
A program may use at most 128 MiB of HBM per device.

v0:
```python
import jax
import jax.numpy as jnp
from jax import lax
from jax.sharding import PartitionSpec as P

CAP = 2


def per_device(
    states, lengths, assign, norm_gain, gate_weight, up_weight, down_weight, out_gain, centroids
):
    passes, seq, width_part = states.shape
    whole = lax.all_gather(states, "tensor", axis=2, tiled=True)
    width = whole.shape[2]
    rows_n = passes * seq
    flat = whole.reshape(rows_n, width).astype(jnp.float32)
    scale = lax.rsqrt(jnp.mean(flat * flat, axis=1, keepdims=True) + 1e-05)
    normed = (flat * scale * norm_gain[None, :]).astype(jnp.bfloat16)
    gate = jnp.dot(
        normed,
        lax.all_gather(gate_weight, "list", axis=0, tiled=True),
        preferred_element_type=jnp.float32,
    )
    up = jnp.dot(
        normed,
        lax.all_gather(up_weight, "list", axis=0, tiled=True),
        preferred_element_type=jnp.float32,
    )
    hidden = (jax.nn.silu(gate) * up).astype(jnp.bfloat16)
    slots = jnp.arange(seq, dtype=jnp.int32)
    valid = (slots[None, :] < lengths[:, None]).astype(jnp.float32)
    pool_w = valid / lengths[:, None].astype(jnp.float32)
    own_states = states.astype(jnp.float32)
    terms = jnp.dot(
        hidden,
        lax.all_gather(down_weight, "list", axis=1, tiled=True),
        preferred_element_type=jnp.float32,
    )
    mixed = lax.psum_scatter(terms, "tensor", scatter_dimension=1, tiled=True)
    layer = own_states + mixed.reshape(passes, seq, width_part)
    pooled = jnp.einsum("ps,psd->pd", pool_w, layer)
    total = lax.psum(jnp.sum(pooled * pooled, axis=1), "tensor")
    embedding = pooled * lax.rsqrt(total[:, None] / width + 1e-05) * out_gain[None, :]
    n_list = lax.axis_size("list")
    per_owner = centroids.shape[0]
    owner = assign // per_owner
    local_id = assign - owner * per_owner
    places = jnp.arange(passes, dtype=jnp.int32)
    same_owner = owner[:, None] == owner[None, :]
    earlier = places[:, None] > places[None, :]
    rank = jnp.sum((same_owner & earlier).astype(jnp.int32), axis=1)
    owner_hit = owner[None, None, :] == jnp.arange(n_list, dtype=jnp.int32)[:, None, None]
    slot_hit = rank[None, None, :] == jnp.arange(CAP, dtype=jnp.int32)[None, :, None]
    select_int = (owner_hit & slot_hit).astype(jnp.int32)
    select = select_int.astype(jnp.float32)
    send_id = jnp.sum(select_int * local_id[None, None, :], axis=2)
    send_rows = jnp.einsum("ocp,pd->ocd", select, embedding, precision=lax.Precision.HIGHEST)
    got_rows = lax.all_to_all(send_rows, "list", split_axis=0, concat_axis=0, tiled=True)
    got_id = lax.all_to_all(send_id, "list", split_axis=0, concat_axis=0, tiled=True)
    differences = got_rows - jnp.take(centroids, got_id, axis=0).astype(jnp.float32)
    returned = lax.all_to_all(differences, "list", split_axis=0, concat_axis=0, tiled=True)
    residual = jnp.einsum("ocp,ocd->pd", select, returned, precision=lax.Precision.HIGHEST)
    return (embedding, residual)


def solution(mesh):
    return jax.shard_map(
        per_device,
        mesh=mesh,
        in_specs=(
            P("list", None, "tensor"),
            P("list"),
            P("list"),
            P(),
            P("list", "tensor"),
            P("list", "tensor"),
            P("tensor", "list"),
            P("tensor"),
            P("list", "tensor"),
        ),
        out_specs=(P("list", "tensor"), P("list", "tensor")),
        check_vma=False,
    )
```

profile of v0, /device:TPU:1, one launch (start us, length us, event | category | flops | bytes accessed | tf_op | source)
XLA Modules:
  0.0 559.1 jit_solution(4250680985617438824)
XLA Ops:
  7.2 0.0 copy-start.4
  7.2 0.0 all-gather.5.cloned.1.call-start
  7.2 0.7 all-gather.5.cloned.1.call-update
  7.9 0.0 all-gather.7.cloned.1.call-start
  8.0 0.7 all-gather.7.cloned.1.call-update
  8.7 0.0 all-gather.11.cloned.1.call-start
  8.7 0.7 all-gather.11.cloned.1.call-update
  9.4 0.0 all-gather.9.cloned.1.call-start
  9.4 0.5 all-gather.9.cloned.1.call-update
  10.0 0.0 reduce-scatter.2.cloned.1.call-start
  10.0 97.2 %all-gather.5.cloned.1.call-done = bf16[24,16,4096]{2,1,0:T(8,128)(2,1)} async-done(((bf16[24,16,512]{2,1,0:T(8,128)(2,1)}), bf16[24,16,4096]{2,1,0:T(8,128)(2,1)}) %all-gather.5.cloned.1.call-update) | async-done | bytes 3145744 | tf_op jit(solution)/shard_map/all_gather | solution.py:13
  107.2 0.0 copy-start
  107.2 2.7 multiply_reduce_fusion
  109.9 0.1 rsqrt.16
  110.0 0.0 copy-done.4
  110.0 0.0 copy-done
  110.0 2.7 fusion.1
  112.8 0.0 copy-start.1
  112.8 61.6 %all-gather.7.cloned.1.call-done = bf16[4096,896]{1,0:T(8,128)(2,1)} async-done(((bf16[128,896]{1,0:T(8,128)(2,1)}), bf16[4096,896]{1,0:T(8,128)(2,1)}) %all-gather.7.cloned.1.call-update) | async-done | bytes 7340048 | tf_op jit(solution)/shard_map/all_gather | solution.py:21
  174.4 8.6 %fusion.22 = f32[384,896]{1,0:T(8,128)} fusion(bf16[384,4096]{1,0:T(8,128)(2,1)} %fusion.1, bf16[4096,896]{1,0:T(8,128)(2,1)} %all-gather.7.cloned.1.call-done), kind=kOutput, calls=%fused_computation.48 | convolution fusion | flops 2818572288 | bytes 11862016 | tf_op jit(solution)/shard_map/dot_general | solution.py:19
  183.0 75.2 %all-gather.11.cloned.1.call-done = bf16[896,4096]{1,0:T(8,128)(2,1)} async-done(((bf16[896,128]{1,0:T(8,128)(2,1)}), bf16[896,4096]{1,0:T(8,128)(2,1)}) %all-gather.11.cloned.1.call-update) | async-done | bytes 7340048 | tf_op jit(solution)/shard_map/all_gather | solution.py:36
  258.2 68.5 %all-gather.9.cloned.1.call-done = bf16[4096,896]{1,0:T(8,128)(2,1)} async-done(((bf16[128,896]{1,0:T(8,128)(2,1)}), bf16[4096,896]{1,0:T(8,128)(2,1)}) %all-gather.9.cloned.1.call-update) | async-done | bytes 7340048 | tf_op jit(solution)/shard_map/all_gather | solution.py:26
  326.7 0.0 copy-done.1
  326.7 14.9 %fusion.6 = f32[384,4096]{1,0:T(8,128)} fusion(bf16[896,4096]{1,0:T(8,128)(2,1)} %all-gather.11.cloned.1.call-done, bf16[384,4096]{1,0:T(8,128)(2,1)S(1)} %copy-done.1, bf16[4096,896]{1,0:T(8,128)(2,1)} %all-gather.9.cloned.1.call-done, f32[384,896]{1,0:T(8,128)} %fusion.22), kind=kOutput, calls=%fused_computation.11 | convolution fusion | flops 5639208960 | bytes 25493504 | tf_op jit(solution)/shard_map/dot_general | solution.py:34
  341.5 0.0 copy-start.7
  341.5 0.0 copy-start.6
  341.6 0.0 copy-start.2
  341.6 0.0 copy-start.5
  341.6 0.0 reduce-scatter.2.cloned.1.call-update
  341.6 0.6 copy-done.7
  342.2 0.2 convert_reduce_fusion
  342.4 0.1 iota_compare_fusion.1
  342.5 0.1 fusion.15
  342.6 0.7 copy.22
  343.3 5.2 all-to-all-start.1
  348.4 0.0 copy-done.6
  348.5 0.1 convert_divide_fusion
  348.5 7.1 %all-to-all-done.1 = s32[32,1,2]{2,1,0:T(1,128)S(1)} async-done(((s32[32,1,2]{2,1,0:T(1,128)}), s32[32,1,2]{2,1,0:T(1,128)S(1)}, u32[]{:S(2)}, u32[]{:S(2)}) %all-to-all-start.1) | async-done | bytes 288 | tf_op jit(solution)/shard_map/all_to_all | solution.py:59
  355.7 0.1 copy.23
  355.8 0.1 copy.26
  355.9 0.1 reshape.125
  356.0 137.2 %reduce-scatter.2.cloned.1.call-done = f32[384,512]{1,0:T(8,128)} async-done(((f32[384,4096]{1,0:T(8,128)}), f32[384,512]{1,0:T(8,128)}) %reduce-scatter.2.cloned.1.call-update) | async-done | bytes 786448 | tf_op jit(solution)/shard_map/reduce_scatter | solution.py:39
  493.2 0.0 copy-done.2
  493.2 1.3 fusion.3
  494.5 0.1 fusion.10
  494.6 20.4 %psum.7 = f32[24]{0:T(128)S(1)} all-reduce(f32[24]{0:T(128)S(1)} %fusion.10), channel_id=1, replica_groups=mesh['list'=32,'tensor'=8] {'tensor'}, use_global_device_ids=true, to_apply=%region_3.4 | all-reduce | flops 24 | bytes 192 | tf_op jit(solution)/shard_map/psum | solution.py:42
  515.0 0.0 copy-done.5
  515.0 0.1 fusion.11
  515.1 0.0 copy-start.3
  515.1 0.4 fusion.8
  515.5 0.7 copy.21
  516.2 14.5 %all-to-all-start = ((f32[32,2,512]{2,1,0:T(2,128)}), f32[32,2,512]{2,1,0:T(2,128)S(1)}, u32[]{:S(2)}, u32[]{:S(2)}) async-start(f32[32,2,512]{2,1,0:T(2,128)} %copy.21), calls=%async_computation.1 | async-start | bytes 262144 | tf_op jit(solution)/shard_map/all_to_all | solution.py:58
  530.8 3.4 gather_fusion
  534.3 0.1 copy.24
  534.4 4.9 all-to-all-done
  539.3 0.1 convert_subtract_fusion
  539.5 12.1 %all_to_all.25 = f32[32,2,512]{2,1,0:T(2,128)S(1)} all-to-all(f32[32,2,512]{2,1,0:T(2,128)S(1)} %convert_subtract_fusion), channel_id=1, replica_groups=mesh['list'=32,'tensor'=8] {'list'}, dimensions={0} | all-to-all | bytes 262144 | tf_op jit(solution)/shard_map/all_to_all | solution.py:61
  551.6 0.9 convolution_bitcast_fusion
  552.5 0.0 copy-done.3
  (9 shorter events, 0.1 us)
Async XLA Ops:
  7.2 102.9 %copy-start.4 = (f32[4096]{0:T(1024)S(1)}, f32[4096]{0:T(1024)}, u32[]{:S(2)}) copy-start(f32[4096]{0:T(1024)} %param.12) | copy-start | bytes 49156
  7.2 100.0 %all-gather.5.cloned.1.call-start = ((), (), s32[]{:S(2)}) async-start(), calls=%async_computation.4 | async-start | bytes 3538944 | tf_op jit(solution)/shard_map/all_gather | solution.py:13
  7.9 166.4 %all-gather.7.cloned.1.call-start = ((), (), s32[]{:S(2)}) async-start(), calls=%async_computation.5 | async-start | bytes 7569408 | tf_op jit(solution)/shard_map/all_gather | solution.py:21
  8.7 249.5 %all-gather.11.cloned.1.call-start = ((), (), s32[]{:S(2)}) async-start(), calls=%async_computation.7 | async-start | bytes 7569408 | tf_op jit(solution)/shard_map/all_gather | solution.py:36
  9.4 317.3 %all-gather.9.cloned.1.call-start = ((), (), s32[]{:S(2)}) async-start(), calls=%async_computation.6 | async-start | bytes 7569408 | tf_op jit(solution)/shard_map/all_gather | solution.py:26
  10.0 483.2 %reduce-scatter.2.cloned.1.call-start = ((), (), s32[]{:S(2)}) async-start(), calls=%async_computation.8 | async-start | bytes 7077888 | tf_op jit(solution)/shard_map/reduce_scatter | solution.py:39
  107.2 2.8 copy-start
  112.8 213.9 %copy-start.1 = (bf16[384,4096]{1,0:T(8,128)(2,1)S(1)}, bf16[384,4096]{1,0:T(8,128)(2,1)}, u32[]{:S(2)}) copy-start(bf16[384,4096]{1,0:T(8,128)(2,1)} %fusion.1) | copy-start | bytes 9437188
  341.5 0.7 copy-start.7
  341.5 6.9 %copy-start.6 = (s32[24]{0:T(128)S(1)}, s32[24]{0:T(128)}, u32[]{:S(2)}) copy-start(s32[24]{0:T(128)} %param.10) | copy-start | bytes 292
  341.6 151.6 %copy-start.2 = (bf16[24,16,512]{2,1,0:T(8,128)(2,1)S(1)}, bf16[24,16,512]{2,1,0:T(8,128)(2,1)}, u32[]{:S(2)}) copy-start(bf16[24,16,512]{2,1,0:T(8,128)(2,1)} %param.9) | copy-start | bytes 1179652
  341.6 173.5 %copy-start.5 = (f32[512]{0:T(512)S(1)}, f32[512]{0:T(512)}, u32[]{:S(2)}) copy-start(f32[512]{0:T(512)} %param.16) | copy-start | bytes 6148
  343.3 12.4 %all-to-all-start.1 = ((s32[32,1,2]{2,1,0:T(1,128)}), s32[32,1,2]{2,1,0:T(1,128)S(1)}, u32[]{:S(2)}, u32[]{:S(2)}) async-start(s32[32,1,2]{2,1,0:T(1,128)} %copy.22), calls=%async_computation.2 | async-start | bytes 32768 | tf_op jit(solution)/shard_map/all_to_all | solution.py:59
  515.1 37.4 %copy-start.3 = (f32[24,512]{1,0:T(8,128)}, f32[24,512]{1,0:T(8,128)S(1)}, u32[]{:S(2)}) copy-start(f32[24,512]{1,0:T(8,128)S(1)} %fusion.11) | copy-start | bytes 147460
  516.2 23.1 %all-to-all-start = ((f32[32,2,512]{2,1,0:T(2,128)}), f32[32,2,512]{2,1,0:T(2,128)S(1)}, u32[]{:S(2)}, u32[]{:S(2)}) async-start(f32[32,2,512]{2,1,0:T(2,128)} %copy.21), calls=%async_computation.1 | async-start | bytes 262144 | tf_op jit(solution)/shard_map/all_to_all | solution.py:58
Sparse Core Ops, SparseCore 0:
  10.5 96.6 all-gather.4
  109.1 65.2 all-gather.6
  176.1 81.9 all-gather.10
  259.9 66.7 all-gather.8
  341.7 151.4 reduce-scatter.1
where the time goes:
time: 559 us
  waiting for transfers between devices  454 us (81%)
  blocking collectives  32.5 us (6%)
  matrix products  26.1 us (5%)
  starting transfers between devices  19.9 us (4%)
  between operations  13.9 us (2%)
  other arithmetic  6.25 us (1%)
  local copies, waits for them, and re-layouts  6.05 us (1%)
    reduce_scatter x1, waiting for transfers between devices, per_device(): mixed = lax.psum_scatter(terms, 'tensor', scatter_dimension=1, tiled=True)  137 us
    all_gather x1, waiting for transfers between devices, per_device(): whole = lax.all_gather(states, 'tensor', axis=2, tiled=True)  97.2 us
    all_gather x1, waiting for transfers between devices, per_device(): lax.all_gather(down_weight, 'list', axis=1, tiled=True)  75.2 us
    all_gather x1, waiting for transfers between devices, per_device(): lax.all_gather(up_weight, 'list', axis=0, tiled=True)  68.5 us
    all_gather x1, waiting for transfers between devices, per_device(): lax.all_gather(gate_weight, 'list', axis=0, tiled=True)  61.6 us
    psum x1, blocking collectives, per_device(): total = lax.psum(jnp.sum(pooled * pooled, axis=1), 'tensor')  20.4 us
    dot_general x1, matrix products, per_device(): jnp.dot(hidden, lax.all_gather(down_weight, 'list', axis=1, tiled=True),...  14.9 us
    all_to_all x1, starting transfers between devices, per_device(): lax.all_to_all(send_rows, 'list', split_axis=0, concat_axis=0, tiled=True)  14.5 us
  transfers between devices with their start and end apart: 7, of which 7 were waited for; matrix products, arithmetic and copies ran while one was open for 3% of the time, Pallas kernels for 0%

commit v1 on v0

--- a/solution.py
+++ b/solution.py
@@ -39,7 +39,7 @@
     mixed = lax.psum_scatter(terms, "tensor", scatter_dimension=1, tiled=True)
     layer = own_states + mixed.reshape(passes, seq, width_part)
     pooled = jnp.einsum("ps,psd->pd", pool_w, layer)
-    total = lax.psum(jnp.sum(pooled * pooled, axis=1), "tensor")
+    total = jnp.sum(lax.all_gather(jnp.sum(pooled * pooled, axis=1), "tensor"), axis=0)
     embedding = pooled * lax.rsqrt(total[:, None] / width + 1e-05) * out_gain[None, :]
     n_list = lax.axis_size("list")
     per_owner = centroids.shape[0]

time: 559 us -> 560 us (level)
    psum x1 -> x0, blocking collectives: 20.4 us -> none  [per_device(): total = lax.psum(jnp.sum(pooled * pooled, axis=1), 'tensor')]
    unnamed x0 -> x1, blocking collectives: none -> 20.4 us
    all_gather x1, waiting for transfers between devices: 75.2 us -> 83.7 us  [per_device(): lax.all_gather(down_weight, 'list', axis=1, tiled=True)]
    all_gather x1, waiting for transfers between devices: 68.5 us -> 60.2 us  [per_device(): lax.all_gather(up_weight, 'list', axis=0, tiled=True)]
  transfers between devices with their start and end apart: 7 -> 7, of which waited for: 7 -> 7; matrix products, arithmetic and copies ran while one was open for 3% -> 4% of each run, Pallas kernels for 0% -> 0%
where the time goes in v1:
time: 560 us; the launch traced here: 559 us
  waiting for transfers between devices  453 us (81%)
  blocking collectives  32.5 us (6%)
  matrix products  26.1 us (5%)
  starting transfers between devices  19.8 us (4%)
  between operations  14.6 us (3%)
  local copies, waits for them, and re-layouts  6.96 us (1%)
  other arithmetic  6.28 us (1%)
    reduce_scatter x1, waiting for transfers between devices, per_device(): mixed = lax.psum_scatter(terms, 'tensor', scatter_dimension=1, tiled=True)  137 us
    all_gather x1, waiting for transfers between devices, per_device(): whole = lax.all_gather(states, 'tensor', axis=2, tiled=True)  97.2 us
    all_gather x1, waiting for transfers between devices, per_device(): lax.all_gather(down_weight, 'list', axis=1, tiled=True)  83.7 us
    all_gather x1, waiting for transfers between devices, per_device(): lax.all_gather(gate_weight, 'list', axis=0, tiled=True)  61.6 us
    all_gather x1, waiting for transfers between devices, per_device(): lax.all_gather(up_weight, 'list', axis=0, tiled=True)  60.2 us
    unnamed x1, blocking collectives  20.4 us
    dot_general x1, matrix products, per_device(): jnp.dot(hidden, lax.all_gather(down_weight, 'list', axis=1, tiled=True),...  14.9 us
    all_to_all x1, starting transfers between devices, per_device(): lax.all_to_all(send_rows, 'list', split_axis=0, concat_axis=0, tiled=True)  14.5 us
  transfers between devices with their start and end apart: 7, of which 7 were waited for; matrix products, arithmetic and copies ran while one was open for 4% of the time, Pallas kernels for 0%

profile of v1, /device:TPU:1, one launch (start us, length us, event | category | flops | bytes accessed | tf_op | source)
XLA Modules:
  0.0 559.2 jit_solution(9661596571127909584)
XLA Ops:
  7.2 0.0 copy-start.4
  7.2 0.0 all-gather.6.cloned.1.call-start
  7.2 0.7 all-gather.6.cloned.1.call-update
  7.9 0.0 all-gather.8.cloned.1.call-start
  8.0 0.7 all-gather.8.cloned.1.call-update
  8.7 0.0 all-gather.10.cloned.1.call-start
  8.7 0.7 all-gather.10.cloned.1.call-update
  9.4 0.0 all-gather.12.cloned.1.call-start
  9.4 0.5 all-gather.12.cloned.1.call-update
  10.0 0.0 reduce-scatter.2.cloned.1.call-start
  10.0 97.2 %all-gather.6.cloned.1.call-done = bf16[24,16,4096]{2,1,0:T(8,128)(2,1)} async-done(((bf16[24,16,512]{2,1,0:T(8,128)(2,1)}), bf16[24,16,4096]{2,1,0:T(8,128)(2,1)}) %all-gather.6.cloned.1.call-update) | async-done | bytes 3145744 | tf_op jit(solution)/shard_map/all_gather | solution.py:13
  107.2 0.0 copy-start
  107.2 2.7 multiply_reduce_fusion
  109.9 0.1 rsqrt.20
  110.0 0.0 copy-done.4
  110.0 0.0 copy-done
  110.0 2.7 fusion.1
  112.8 0.0 copy-start.1
  112.8 61.6 %all-gather.8.cloned.1.call-done = bf16[4096,896]{1,0:T(8,128)(2,1)} async-done(((bf16[128,896]{1,0:T(8,128)(2,1)}), bf16[4096,896]{1,0:T(8,128)(2,1)}) %all-gather.8.cloned.1.call-update) | async-done | bytes 7340048 | tf_op jit(solution)/shard_map/all_gather | solution.py:21
  174.4 8.6 %fusion.22 = f32[384,896]{1,0:T(8,128)} fusion(bf16[384,4096]{1,0:T(8,128)(2,1)} %fusion.1, bf16[4096,896]{1,0:T(8,128)(2,1)} %all-gather.8.cloned.1.call-done), kind=kOutput, calls=%fused_computation.48 | convolution fusion | flops 2818572288 | bytes 11862016 | tf_op jit(solution)/shard_map/dot_general | solution.py:19
  183.0 60.2 %all-gather.10.cloned.1.call-done = bf16[4096,896]{1,0:T(8,128)(2,1)} async-done(((bf16[128,896]{1,0:T(8,128)(2,1)}), bf16[4096,896]{1,0:T(8,128)(2,1)}) %all-gather.10.cloned.1.call-update) | async-done | bytes 7340048 | tf_op jit(solution)/shard_map/all_gather | solution.py:26
  243.2 83.7 %all-gather.12.cloned.1.call-done = bf16[896,4096]{1,0:T(8,128)(2,1)} async-done(((bf16[896,128]{1,0:T(8,128)(2,1)}), bf16[896,4096]{1,0:T(8,128)(2,1)}) %all-gather.12.cloned.1.call-update) | async-done | bytes 7340048 | tf_op jit(solution)/shard_map/all_gather | solution.py:36
  326.8 0.0 copy-done.1
  326.8 14.9 %fusion.6 = f32[384,4096]{1,0:T(8,128)} fusion(bf16[896,4096]{1,0:T(8,128)(2,1)} %all-gather.12.cloned.1.call-done, bf16[384,4096]{1,0:T(8,128)(2,1)S(1)} %copy-done.1, bf16[4096,896]{1,0:T(8,128)(2,1)} %all-gather.10.cloned.1.call-done, f32[384,896]{1,0:T(8,128)} %fusion.22), kind=kOutput, calls=%fused_computation.11 | convolution fusion | flops 5639208960 | bytes 25493504 | tf_op jit(solution)/shard_map/dot_general | solution.py:34
  341.7 0.0 copy-start.7
  341.7 0.0 copy-start.6
  341.7 0.0 copy-start.8
  341.7 0.0 copy-start.2
  341.7 0.0 copy-start.5
  341.7 0.0 reduce-scatter.2.cloned.1.call-update
  341.8 0.6 copy-done.7
  342.4 0.2 convert_reduce_fusion
  342.6 0.1 iota_compare_fusion.1
  342.6 0.1 fusion.15
  342.7 0.7 copy.22
  343.4 5.1 all-to-all-start.1
  348.5 0.0 copy-done.6
  348.5 0.1 convert_divide_fusion
  348.6 0.0 copy-done.8
  348.6 0.6 dynamic-slice
  349.9 5.9 %all-to-all-done.1 = s32[32,1,2]{2,1,0:T(1,128)S(1)} async-done(((s32[32,1,2]{2,1,0:T(1,128)}), s32[32,1,2]{2,1,0:T(1,128)S(1)}, u32[]{:S(2)}, u32[]{:S(2)}) %all-to-all-start.1) | async-done | bytes 288 | tf_op jit(solution)/shard_map/all_to_all | solution.py:59
  355.7 0.1 copy.23
  355.8 0.1 copy.26
  355.9 0.1 reshape.129
  356.0 137.0 %reduce-scatter.2.cloned.1.call-done = f32[384,512]{1,0:T(8,128)} async-done(((f32[384,4096]{1,0:T(8,128)}), f32[384,512]{1,0:T(8,128)}) %reduce-scatter.2.cloned.1.call-update) | async-done | bytes 786448 | tf_op jit(solution)/shard_map/reduce_scatter | solution.py:39
  493.0 0.0 copy-done.2
  493.0 1.3 fusion.3
  494.3 0.1 fusion.10
  494.5 0.2 dynamic-update-slice
  494.7 20.4 %all-reduce = f32[192]{0:T(256)S(1)} all-reduce(f32[192]{0:T(256)S(1)} %dynamic-update-slice), channel_id=2, replica_groups=mesh['list'=32,'tensor'=8] {'tensor'}, use_global_device_ids=true, to_apply=%add | all-reduce | flops 192 | bytes 1536
  515.1 0.1 reshape.135
  515.2 0.0 copy-done.5
  515.2 0.1 fusion.11
  515.2 0.0 copy-start.3
  515.3 0.4 fusion.8
  515.6 0.8 copy.21
  516.4 14.5 %all-to-all-start = ((f32[32,2,512]{2,1,0:T(2,128)}), f32[32,2,512]{2,1,0:T(2,128)S(1)}, u32[]{:S(2)}, u32[]{:S(2)}) async-start(f32[32,2,512]{2,1,0:T(2,128)} %copy.21), calls=%async_computation.1 | async-start | bytes 262144 | tf_op jit(solution)/shard_map/all_to_all | solution.py:58
  531.0 3.4 gather_fusion
  534.4 0.1 copy.24
  534.6 4.9 all-to-all-done
  539.5 0.1 convert_subtract_fusion
  539.6 12.1 %all_to_all.25 = f32[32,2,512]{2,1,0:T(2,128)S(1)} all-to-all(f32[32,2,512]{2,1,0:T(2,128)S(1)} %convert_subtract_fusion), channel_id=1, replica_groups=mesh['list'=32,'tensor'=8] {'list'}, dimensions={0} | all-to-all | bytes 262144 | tf_op jit(solution)/shard_map/all_to_all | solution.py:61
  551.8 0.9 convolution_bitcast_fusion
  552.7 0.0 copy-done.3
  (11 shorter events, 0.1 us)
Async XLA Ops:
  7.2 102.9 %copy-start.4 = (f32[4096]{0:T(1024)S(1)}, f32[4096]{0:T(1024)}, u32[]{:S(2)}) copy-start(f32[4096]{0:T(1024)} %param.12) | copy-start | bytes 49156
  7.2 100.0 %all-gather.6.cloned.1.call-start = ((), (), s32[]{:S(2)}) async-start(), calls=%async_computation.4 | async-start | bytes 3538944 | tf_op jit(solution)/shard_map/all_gather | solution.py:13
  7.9 166.4 %all-gather.8.cloned.1.call-start = ((), (), s32[]{:S(2)}) async-start(), calls=%async_computation.5 | async-start | bytes 7569408 | tf_op jit(solution)/shard_map/all_gather | solution.py:21
  8.7 234.5 %all-gather.10.cloned.1.call-start = ((), (), s32[]{:S(2)}) async-start(), calls=%async_computation.6 | async-start | bytes 7569408 | tf_op jit(solution)/shard_map/all_gather | solution.py:26
  9.4 317.4 %all-gather.12.cloned.1.call-start = ((), (), s32[]{:S(2)}) async-start(), calls=%async_computation.7 | async-start | bytes 7569408 | tf_op jit(solution)/shard_map/all_gather | solution.py:36
  10.0 483.0 %reduce-scatter.2.cloned.1.call-start = ((), (), s32[]{:S(2)}) async-start(), calls=%async_computation.8 | async-start | bytes 7077888 | tf_op jit(solution)/shard_map/reduce_scatter | solution.py:39
  107.2 2.8 copy-start
  112.8 214.1 %copy-start.1 = (bf16[384,4096]{1,0:T(8,128)(2,1)S(1)}, bf16[384,4096]{1,0:T(8,128)(2,1)}, u32[]{:S(2)}) copy-start(bf16[384,4096]{1,0:T(8,128)(2,1)} %fusion.1) | copy-start | bytes 9437188
  341.7 0.7 copy-start.7
  341.7 6.8 %copy-start.6 = (s32[24]{0:T(128)S(1)}, s32[24]{0:T(128)}, u32[]{:S(2)}) copy-start(s32[24]{0:T(128)} %param.10) | copy-start | bytes 292
  341.7 6.9 %copy-start.8 = (u32[256]{0:T(256)S(1)}, u32[256]{0:T(256)}, u32[]{:S(2)}) copy-start(u32[256]{0:T(256)} %constant.51) | copy-start | bytes 3076
  341.7 151.3 %copy-start.2 = (bf16[24,16,512]{2,1,0:T(8,128)(2,1)S(1)}, bf16[24,16,512]{2,1,0:T(8,128)(2,1)}, u32[]{:S(2)}) copy-start(bf16[24,16,512]{2,1,0:T(8,128)(2,1)} %param.9) | copy-start | bytes 1179652
  341.7 173.4 %copy-start.5 = (f32[512]{0:T(512)S(1)}, f32[512]{0:T(512)}, u32[]{:S(2)}) copy-start(f32[512]{0:T(512)} %param.16) | copy-start | bytes 6148
  343.4 12.3 %all-to-all-start.1 = ((s32[32,1,2]{2,1,0:T(1,128)}), s32[32,1,2]{2,1,0:T(1,128)S(1)}, u32[]{:S(2)}, u32[]{:S(2)}) async-start(s32[32,1,2]{2,1,0:T(1,128)} %copy.22), calls=%async_computation.2 | async-start | bytes 32768 | tf_op jit(solution)/shard_map/all_to_all | solution.py:59
  515.2 37.4 %copy-start.3 = (f32[24,512]{1,0:T(8,128)}, f32[24,512]{1,0:T(8,128)S(1)}, u32[]{:S(2)}) copy-start(f32[24,512]{1,0:T(8,128)S(1)} %fusion.11) | copy-start | bytes 147460
  516.4 23.1 %all-to-all-start = ((f32[32,2,512]{2,1,0:T(2,128)}), f32[32,2,512]{2,1,0:T(2,128)S(1)}, u32[]{:S(2)}, u32[]{:S(2)}) async-start(f32[32,2,512]{2,1,0:T(2,128)} %copy.21), calls=%async_computation.1 | async-start | bytes 262144 | tf_op jit(solution)/shard_map/all_to_all | solution.py:58
Sparse Core Ops, SparseCore 0:
  10.5 96.6 all-gather.5
  109.1 65.2 all-gather.7
  176.2 66.9 all-gather.9
  244.8 81.9 all-gather.11
  341.9 151.0 reduce-scatter.1
